TPU v7x, 32 devices: a whole 2x2x4 slice. The times are simulated.
32 devices in a mesh: gx: 8 (over y, x, core), gy: 4 (over z).
Axes of the slice: x: 2, y: 2, z: 4, core: 2. Of those that a mesh axis runs over, the one named last changes fastest.
Arguments:
- nest_fields: float32 [5, 80, 24, 1536], P(None, None, 'gx', 'gy'), may hold values from -6 to 6
- boundary_strip: float32 [8, 5, 80, 1536], P('gx', None, None, 'gy'), may hold values from -6 to 6
- strip_owner: int32 [4], replicated, may hold values from 0 to 7, as said below
- terrain_slope: float32 [24, 1536], P('gx', 'gy'), may hold values from -0.6 to 0.6
- column_metric: float32 [24, 1536], P('gx', 'gy'), may hold values from 0.6 to 1.6
- relax_rate: float32 [24, 1536], P('gx', 'gy'), may hold values from 0.05 to 2
- parent_state: float32 [8, 512, 320], P('gx', 'gy'), may hold values from -6 to 6
- intersection_cell: int32 [8, 4, 4, 4], P('gx', 'gy'), may hold values from 0 to 127
- intersection_row: int32 [8, 4, 4, 4], P('gx', 'gy'), may hold values from 0 to 127
- intersection_count: int32 [8, 4, 4], P('gx', 'gy'), may hold values from 1 to 4, as said below
Outputs:
- nest_out: float32 [5, 80, 24, 1536], P(None, None, 'gx', 'gy')
- parent_out: float32 [8, 512, 320], P('gx', 'gy')
Inputs may be any that keep to these rules, and one draw needn't show every extreme that they name: `strip_owner`: x index that holds the boundary rows of each y block; both 0 and 7 occur. `intersection_count`: at most 4 records go from one device to one y index; in each x group one y index receives 4 records from every device of the group.
All inputs are finite; a program needn't handle non-finite values.
Results may differ from a plain program's by a relative error of at most 0.0003.
Values sent between devices are 32-bit elements; how exact they have to be, the bound alone decides.
A program may use at most 128 MiB of HBM per device.

v0:
```python
import jax
import jax.numpy as jnp
from jax import lax
from jax.sharding import PartitionSpec as P

time_step = 0.25
sound_speed = 1.0
viscosity = 0.05
buoyancy = 0.5
wind_east = 0.6
wind_north = -0.4


def broadcast(value, axis, root):
    mine = lax.axis_index(axis) == root
    return lax.psum(jnp.where(mine, value, jnp.zeros_like(value)), axis)


def padded_2(value, sides, width):
    for axis, dim in sides:
        peers, length = (lax.axis_size(axis), value.shape[dim])
        up = [(i, (i + 1) % peers) for i in range(peers - 1)]
        down = [(j, i) for i, j in up]
        last = lax.slice_in_dim(value, length - width, length, axis=dim)
        leading = lax.slice_in_dim(value, 0, width, axis=dim)
        before = lax.ppermute(last, axis, up)
        after = lax.ppermute(leading, axis, down)
        value = jnp.concatenate([before, value, after], axis=dim)
    return value


def tendency(padded, slope, metric, relax, boundary):
    center = padded[:, :, 1:-1, 1:-1]
    east_cell = padded[:, :, 2:, 1:-1]
    west_cell = padded[:, :, :-2, 1:-1]
    north_cell = padded[:, :, 1:-1, 2:]
    south_cell = padded[:, :, 1:-1, :-2]
    vertical = jnp.pad(center, ((0, 0), (1, 1), (0, 0), (0, 0)))
    along_z = 0.5 * (vertical[:, 2:] - vertical[:, :-2]) * metric
    along_x = 0.5 * (east_cell - west_cell) - slope * along_z
    along_y = 0.5 * (north_cell - south_cell)
    spread = east_cell + west_cell + north_cell + south_cell - 4.0 * center
    common = (
        -(wind_east * along_x + wind_north * along_y)
        + viscosity * spread
        + relax * (boundary[:, :, None, :] - center)
    )
    tend_east = common[0] - sound_speed * along_x[4]
    tend_north = common[1] - sound_speed * along_y[4]
    tend_vert = common[2] - sound_speed * along_z[4] + buoyancy * center[3]
    tend_heat = common[3] - buoyancy * center[2]
    tend_press = common[4] - sound_speed * (along_x[0] + along_y[1] + along_z[2])
    return jnp.stack([tend_east, tend_north, tend_vert, tend_heat, tend_press])


def on_device(
    nest_fields,
    boundary_strip,
    strip_owner,
    terrain_slope,
    column_metric,
    relax_rate,
    parent_state,
    intersection_cell,
    intersection_row,
    intersection_count,
):
    cells_x = nest_fields.shape[2]
    cells_y = nest_fields.shape[3]
    levels = nest_fields.shape[1]
    root_index = strip_owner[lax.axis_index("gy")]
    boundary = broadcast(boundary_strip, "gx", root_index)[0]
    current = nest_fields
    for weight in (1.0 / 3.0, 0.5, 1.0):
        padded = padded_2(current, (("gx", 2), ("gy", 3)), 1)
        current = nest_fields + weight * time_step * tendency(
            padded, terrain_slope, column_metric, relax_rate, boundary
        )
    feedback_fields = jnp.stack([current[0], current[1], current[3], current[4]])
    coarse = feedback_fields.reshape(4, levels, cells_x // 3, 3, cells_y // 3, 3).mean(axis=(3, 5))
    feat_width = 4 * levels
    coarse_table = coarse.transpose(2, 3, 0, 1).reshape(-1, feat_width)
    parent_cells = parent_state.shape[1]
    capacity = intersection_cell.shape[3]
    cell_ids = intersection_cell[0, 0]
    send_counts = intersection_count[0, 0]
    active = jnp.arange(capacity)[None, :] < send_counts[:, None]
    records = coarse_table[cell_ids] * active[..., None].astype(jnp.float32)
    targets = jnp.where(active, intersection_row[0, 0], parent_cells)
    got_values, got_targets = (
        lax.all_to_all(records, "gy", split_axis=0, concat_axis=0, tiled=True),
        lax.all_to_all(targets, "gy", split_axis=0, concat_axis=0, tiled=True),
    )
    flat_values = got_values.reshape(-1, feat_width)
    flat_targets = got_targets.reshape(-1)
    onehot = (flat_targets[None, :] == jnp.arange(parent_cells)[:, None]).astype(jnp.float32)
    totals = jnp.dot(onehot, flat_values, precision=lax.Precision.HIGHEST)
    record_count = jnp.sum(onehot, axis=1)
    parent_rows = parent_state[0]
    merged = jnp.where(
        record_count[:, None] > 0, totals / jnp.maximum(record_count, 1.0)[:, None], parent_rows
    )
    return (current, merged[None])


def solution(mesh):
    placed = (
        P(None, None, "gx", "gy"),
        P("gx", None, None, "gy"),
        P(),
        P("gx", "gy"),
        P("gx", "gy"),
        P("gx", "gy"),
        P("gx", "gy", None),
        P("gx", "gy", None, None),
        P("gx", "gy", None, None),
        P("gx", "gy", None),
    )
    return jax.shard_map(
        on_device,
        mesh=mesh,
        in_specs=placed,
        out_specs=(P(None, None, "gx", "gy"), P("gx", "gy", None)),
        check_vma=False,
    )
```

profile of v0, /device:TPU:6, one launch (start us, length us, event | category | flops | bytes accessed | tf_op | source)
XLA Modules:
  0.0 192.3 jit_solution(10890411660656474874)
XLA Ops:
  7.2 2.4 %fusion.40 = (f32[5,80,1,384]{3,1,2,0:T(8,128)}, f32[5,80,1,384]{3,1,2,0:T(8,128)}) fusion(f32[5,80,3,384]{3,1,2,0:T(8,128)} %param.10), kind=kLoop, calls=%fused_computation.120 | loop fusion | bytes 2457600 | tf_op jit(solution)/shard_map/slice | solution.py:24
  9.6 2.0 %collective-permute-start.1 = (f32[5,80,1,384]{3,1,2,0:T(8,128)}, f32[5,80,1,384]{3,1,2,0:T(8,128)S(1)}, u32[]{:S(2)}, u32[]{:S(2)}) collective-permute-start(f32[5,80,1,384]{3,1,2,0:T(8,128)} %get-tuple-element.26), channel_id=1, source_target_pairs={{0,4},{4,8},{8,12},{12,16},{16,20},{20,24},{24,28},{1,5},{5,9},{9,... | collective-permute-start | bytes 1843208 | tf_op jit(solution)/shard_map/ppermute | solution.py:26
  11.7 3.6 %collective-permute-start = (f32[5,80,1,384]{3,1,2,0:T(8,128)}, f32[5,80,1,384]{3,1,2,0:T(8,128)S(1)}, u32[]{:S(2)}, u32[]{:S(2)}) collective-permute-start(f32[5,80,1,384]{3,1,2,0:T(8,128)} %get-tuple-element.27), channel_id=1, source_target_pairs={{4,0},{8,4},{12,8},{16,12},{20,16},{24,20},{28,24},{5,1},{9,5},{13... | collective-permute-start | bytes 1843208 | tf_op jit(solution)/shard_map/ppermute | solution.py:27
  16.6 0.9 select_bitcast_fusion
  17.5 6.8 %collective-permute-done.1 = f32[5,80,1,384]{3,1,2,0:T(8,128)S(1)} collective-permute-done((f32[5,80,1,384]{3,1,2,0:T(8,128)}, f32[5,80,1,384]{3,1,2,0:T(8,128)S(1)}, u32[]{:S(2)}, u32[]{:S(2)}) %collective-permute-start.1) | collective-permute-done | bytes 614432 | tf_op jit(solution)/shard_map/ppermute | solution.py:26
  24.5 0.8 copy-done.13
  25.3 1.6 fusion.36
  27.3 1.8 copy.68
  29.1 1.3 collective-permute-start.2
  30.4 1.1 copy.69
  31.6 5.1 %collective-permute-start.3 = (f32[5,80,5,1]{1,2,3,0:T(8,128)}, f32[5,80,5,1]{1,2,3,0:T(8,128)}, u32[]{:S(2)}, u32[]{:S(2)}) collective-permute-start(f32[5,80,5,1]{1,2,3,0:T(8,128)} %copy.69), channel_id=1, source_target_pairs={{0,1},{1,2},{2,3},{4,5},{5,6},{6,7},{8,9},{9,10},{10,11},{12,13},{... | collective-permute-start | bytes 24008 | tf_op jit(solution)/shard_map/ppermute | solution.py:26
  37.1 0.7 collective-permute-done.3
  37.8 2.1 %copy.55 = f32[5,80,5,1]{3,1,2,0:T(8,128)} copy(f32[5,80,5,1]{1,2,3,0:T(8,128)} %collective-permute-done.3) | data formatting | bytes 16000 | tf_op jit(solution)/shard_map/ppermute | solution.py:26
  39.9 33.8 %all-reduce.5.cloned.1.call-done = f32[5,80,384]{2,1,0:T(8,128)} async-done(((f32[5,80,384]{2,1,0:T(8,128)}), f32[5,80,384]{2,1,0:T(8,128)}) %all-reduce.5.cloned.1.call-update) | async-done | bytes 614416 | tf_op jit(solution)/shard_map/psum | solution.py:16
  73.6 4.0 %multiply_add_fusion.5 = (f32[5,80,3,384]{3,1,2,0:T(8,128)S(1)}, f32[5,80,3,384]{3,1,2,0:T(8,128)S(1)}, f32[5,80,3,384]{3,1,2,0:T(8,128)S(1)}, f32[5,80,3,384]{3,1,2,0:T(8,128)S(1)}) fusion(f32[5,80,3,384]{3,1,2,0:T(8,128)S(1)} %copy-done, f32[5,80,1,384]{3,1,2,0:T(8,128)} %copy-done.13, f32[5,80,1,384]{3,1,2,0:T(8,128)S(1)} %collective-permute-done.1, ...), kind=kLoop, calls=%fused_computation.40 | loop fusion | flops 11980800 | bytes 14161024 | tf_op jit(solution)/shard_map/add | solution.py:44
  78.3 1.9 collective-permute-start.4
  80.2 2.4 %collective-permute-start.5 = (f32[5,80,1,384]{3,1,2,0:T(8,128)S(1)}, f32[5,80,1,384]{3,1,2,0:T(8,128)S(1)}, u32[]{:S(2)}, u32[]{:S(2)}) collective-permute-start(f32[5,80,1,384]{3,1,2,0:T(8,128)S(1)} %get-tuple-element.24), channel_id=1, source_target_pairs={{0,4},{4,8},{8,12},{12,16},{16,20},{20,24},{24,28},{1,5},{5,9},{9,... | collective-permute-start | bytes 1843208 | tf_op jit(solution)/shard_map/ppermute | solution.py:26
  82.7 5.2 %collective-permute-done.4 = f32[5,80,1,384]{3,1,2,0:T(8,128)S(1)} collective-permute-done((f32[5,80,1,384]{3,1,2,0:T(8,128)S(1)}, f32[5,80,1,384]{3,1,2,0:T(8,128)S(1)}, u32[]{:S(2)}, u32[]{:S(2)}) %collective-permute-start.4) | collective-permute-done | bytes 614432 | tf_op jit(solution)/shard_map/ppermute | solution.py:27
  87.9 8.6 %collective-permute-done.5 = f32[5,80,1,384]{3,1,2,0:T(8,128)S(1)} collective-permute-done((f32[5,80,1,384]{3,1,2,0:T(8,128)S(1)}, f32[5,80,1,384]{3,1,2,0:T(8,128)S(1)}, u32[]{:S(2)}, u32[]{:S(2)}) %collective-permute-start.5) | collective-permute-done | bytes 614432 | tf_op jit(solution)/shard_map/ppermute | solution.py:26
  96.5 1.3 pad_maximum_fusion.23
  97.8 1.7 copy.70
  99.6 1.3 collective-permute-start.6
  100.9 1.1 copy.71
  102.0 5.1 %collective-permute-start.7 = (f32[5,80,5,1]{1,2,3,0:T(8,128)}, f32[5,80,5,1]{1,2,3,0:T(8,128)}, u32[]{:S(2)}, u32[]{:S(2)}) collective-permute-start(f32[5,80,5,1]{1,2,3,0:T(8,128)} %copy.71), channel_id=1, source_target_pairs={{0,1},{1,2},{2,3},{4,5},{5,6},{6,7},{8,9},{9,10},{10,11},{12,13},{... | collective-permute-start | bytes 24008 | tf_op jit(solution)/shard_map/ppermute | solution.py:26
  107.8 3.8 %all-to-all-start = ((s32[4,1,4]{2,1,0:T(1,128)}), s32[4,1,4]{2,1,0:T(1,128)}, u32[]{:S(2)}, u32[]{:S(2)}) async-start(s32[4,1,4]{2,1,0:T(1,128)} %bitcast.4), calls=%async_computation | async-start | bytes 4096 | tf_op jit(solution)/shard_map/all_to_all | solution.py:92
  112.0 2.1 %copy.59 = f32[5,80,5,1]{3,1,2,0:T(8,128)} copy(f32[5,80,5,1]{1,2,3,0:T(8,128)} %collective-permute-done.7) | data formatting | bytes 16000 | tf_op jit(solution)/shard_map/ppermute | solution.py:26
  114.1 7.3 %multiply_add_fusion.3 = (f32[5,80,3,384]{3,1,2,0:T(8,128)S(1)}, f32[5,80,3,384]{3,1,2,0:T(8,128)S(1)}, f32[5,80,3,384]{3,1,2,0:T(8,128)S(1)}) fusion(f32[5,80,3,384]{3,1,2,0:T(8,128)} %copy-done.3, f32[5,80,1,384]{3,1,2,0:T(8,128)S(1)} %collective-permute-done.4, f32[5,80,1,384]{3,1,2,0:T(8,128)} %copy-done.11, ...), kind=kLoop, calls=%fused_computation.37 | loop fusion | flops 13363200 | bytes 9245824 | tf_op jit(solution)/shard_map/add | solution.py:44
  121.5 1.2 broadcast_multiply_fusion.1
  123.2 1.2 copy-done.1
  124.4 1.1 fusion.38
  125.6 1.9 collective-permute-start.8
  127.5 2.4 %collective-permute-start.9 = (f32[5,80,1,384]{3,1,2,0:T(8,128)}, f32[5,80,1,384]{3,1,2,0:T(8,128)S(1)}, u32[]{:S(2)}, u32[]{:S(2)}) collective-permute-start(f32[5,80,1,384]{3,1,2,0:T(8,128)} %get-tuple-element.22), channel_id=1, source_target_pairs={{0,4},{4,8},{8,12},{12,16},{16,20},{20,24},{24,28},{1,5},{5,9},{9,... | collective-permute-start | bytes 1843208 | tf_op jit(solution)/shard_map/ppermute | solution.py:26
  130.6 1.3 reduce.6
  132.2 3.3 %collective-permute-done.8 = f32[5,80,1,384]{3,1,2,0:T(8,128)S(1)} collective-permute-done((f32[5,80,1,384]{3,1,2,0:T(8,128)}, f32[5,80,1,384]{3,1,2,0:T(8,128)S(1)}, u32[]{:S(2)}, u32[]{:S(2)}) %collective-permute-start.8) | collective-permute-done | bytes 614432 | tf_op jit(solution)/shard_map/ppermute | solution.py:27
  135.4 8.3 %collective-permute-done.9 = f32[5,80,1,384]{3,1,2,0:T(8,128)S(1)} collective-permute-done((f32[5,80,1,384]{3,1,2,0:T(8,128)}, f32[5,80,1,384]{3,1,2,0:T(8,128)S(1)}, u32[]{:S(2)}, u32[]{:S(2)}) %collective-permute-start.9) | collective-permute-done | bytes 614432 | tf_op jit(solution)/shard_map/ppermute | solution.py:26
  143.8 3.2 %pad_maximum_fusion.20 = (f32[5,80,5,1]{3,1,2,0:T(8,128)}, f32[5,80,5,1]{3,1,2,0:T(8,128)}) fusion(f32[5,80,1,384]{3,1,2,0:T(8,128)S(1)} %collective-permute-done.8, f32[5,80,3,384]{3,1,2,0:T(8,128)} %copy-done.1, f32[5,80,1,384]{3,1,2,0:T(8,128)S(1)} %collective-permute-done.9), kind=kLoop, calls=%fused_computation.46 | loop fusion | flops 8000 | bytes 3088000 | tf_op jit(solution)/shard_map/concatenate | solution.py:28
  147.0 1.7 copy.72
  148.7 1.3 collective-permute-start.10
  150.0 1.7 copy.73
  151.7 5.2 %collective-permute-start.11 = (f32[5,80,5,1]{1,2,3,0:T(8,128)S(1)}, f32[5,80,5,1]{1,2,3,0:T(8,128)}, u32[]{:S(2)}, u32[]{:S(2)}) collective-permute-start(f32[5,80,5,1]{1,2,3,0:T(8,128)S(1)} %copy.73), channel_id=1, source_target_pairs={{0,1},{1,2},{2,3},{4,5},{5,6},{6,7},{8,9},{9,10},{10,11},{12,13},{... | collective-permute-start | bytes 24008 | tf_op jit(solution)/shard_map/ppermute | solution.py:26
  157.9 2.1 %copy.63 = f32[5,80,5,1]{3,1,2,0:T(8,128)} copy(f32[5,80,5,1]{1,2,3,0:T(8,128)} %collective-permute-done.11) | data formatting | bytes 16000 | tf_op jit(solution)/shard_map/ppermute | solution.py:26
  160.0 7.3 %multiply_add_fusion.1 = (f32[5,80,3,384]{3,1,2,0:T(8,128)S(1)}, f32[5,80,3,384]{3,1,2,0:T(8,128)S(1)}, f32[5,80,3,384]{3,1,2,0:T(8,128)S(1)}) fusion(f32[5,80,3,384]{3,1,2,0:T(8,128)} %copy-done.1, f32[5,80,1,384]{3,1,2,0:T(8,128)S(1)} %collective-permute-done.8, f32[5,80,1,384]{3,1,2,0:T(8,128)} %copy-done.9, ...), kind=kLoop, calls=%fused_computation.34 | loop fusion | flops 13363200 | bytes 9245824 | tf_op jit(solution)/shard_map/add | solution.py:44
  167.4 1.2 broadcast_multiply_fusion
  169.1 1.2 copy-done.8
  172.2 0.7 broadcast_multiply_fusion.3
  172.9 5.8 %all-to-all-start.1 = ((f32[4,4,320]{2,1,0:T(4,128)}), f32[4,4,320]{2,1,0:T(4,128)S(1)}, u32[]{:S(2)}, u32[]{:S(2)}) async-start(f32[4,4,320]{2,1,0:T(4,128)} %broadcast_multiply_fusion.3), calls=%async_computation.1 | async-start | bytes 49152 | tf_op jit(solution)/shard_map/all_to_all | solution.py:91
  178.7 5.6 %all-to-all-done.1 = f32[4,4,320]{2,1,0:T(4,128)S(1)} async-done(((f32[4,4,320]{2,1,0:T(4,128)}), f32[4,4,320]{2,1,0:T(4,128)S(1)}, u32[]{:S(2)}, u32[]{:S(2)}) %all-to-all-start.1) | async-done | bytes 20512 | tf_op jit(solution)/shard_map/all_to_all | solution.py:91
  184.4 1.0 fusion.7
  (107 shorter events, 8.1 us)
Async XLA Ops:
  7.2 8.1 %copy-start.23 = (s32[4]{0:T(128)S(1)}, s32[4]{0:T(128)}, u32[]{:S(2)}) copy-start(s32[4]{0:T(128)} %param.12) | copy-start | bytes 52
  7.2 66.4 %all-reduce.5.cloned.1.call-start = ((), (), s32[]{:S(2)}) async-start(), calls=%async_computation.2 | async-start | bytes 1228800 | tf_op jit(solution)/shard_map/psum | solution.py:16
  9.6 14.7 %copy-start = (f32[5,80,3,384]{3,1,2,0:T(8,128)S(1)}, f32[5,80,3,384]{3,1,2,0:T(8,128)}, u32[]{:S(2)}) copy-start(f32[5,80,3,384]{3,1,2,0:T(8,128)} %param.10) | copy-start | bytes 5529604
  9.6 14.7 %collective-permute-start.1 = (f32[5,80,1,384]{3,1,2,0:T(8,128)}, f32[5,80,1,384]{3,1,2,0:T(8,128)S(1)}, u32[]{:S(2)}, u32[]{:S(2)}) collective-permute-start(f32[5,80,1,384]{3,1,2,0:T(8,128)} %get-tuple-element.26), channel_id=1, source_target_pairs={{0,4},{4,8},{8,12},{12,16},{16,20},{20,24},{24,28},{1,5},{5,9},{9,... | collective-permute-start | bytes 1843208 | tf_op jit(solution)/shard_map/ppermute | solution.py:26
  11.7 12.8 %collective-permute-start = (f32[5,80,1,384]{3,1,2,0:T(8,128)}, f32[5,80,1,384]{3,1,2,0:T(8,128)S(1)}, u32[]{:S(2)}, u32[]{:S(2)}) collective-permute-start(f32[5,80,1,384]{3,1,2,0:T(8,128)} %get-tuple-element.27), channel_id=1, source_target_pairs={{4,0},{8,4},{12,8},{16,12},{20,16},{24,20},{28,24},{5,1},{9,5},{13... | collective-permute-start | bytes 1843208 | tf_op jit(solution)/shard_map/ppermute | solution.py:27
  24.5 0.8 copy-start.13
  25.3 2.0 %copy-start.5 = (f32[5,80,5,384]{3,1,2,0:T(8,128)}, f32[5,80,5,384]{3,1,2,0:T(8,128)S(1)}, u32[]{:S(2)}) copy-start(f32[5,80,5,384]{3,1,2,0:T(8,128)S(1)} %constant_dynamic-update-slice_fusion) | copy-start | bytes 9216004
  27.3 9.4 %copy-start.16 = (f32[3,384]{1,0:T(4,128)S(1)}, f32[3,384]{1,0:T(4,128)}, u32[]{:S(2)}) copy-start(f32[3,384]{1,0:T(4,128)} %param.14) | copy-start | bytes 13828
  27.3 46.3 %copy-start.14 = (f32[3,384]{1,0:T(4,128)S(1)}, f32[3,384]{1,0:T(4,128)}, u32[]{:S(2)}) copy-start(f32[3,384]{1,0:T(4,128)} %param.15) | copy-start | bytes 13828
  27.3 46.3 %copy-start.15 = (f32[3,384]{1,0:T(4,128)S(1)}, f32[3,384]{1,0:T(4,128)}, u32[]{:S(2)}) copy-start(f32[3,384]{1,0:T(4,128)} %param.13) | copy-start | bytes 13828
  29.1 7.6 %collective-permute-start.2 = (f32[5,80,5,1]{1,2,3,0:T(8,128)S(1)}, f32[5,80,5,1]{1,2,3,0:T(8,128)S(1)}, u32[]{:S(2)}, u32[]{:S(2)}) collective-permute-start(f32[5,80,5,1]{1,2,3,0:T(8,128)S(1)} %copy.68), channel_id=1, source_target_pairs={{1,0},{2,1},{3,2},{5,4},{6,5},{7,6},{9,8},{10,9},{11,10},{13,12},{... | collective-permute-start | bytes 24008 | tf_op jit(solution)/shard_map/ppermute | solution.py:27
  31.6 6.2 %collective-permute-start.3 = (f32[5,80,5,1]{1,2,3,0:T(8,128)}, f32[5,80,5,1]{1,2,3,0:T(8,128)}, u32[]{:S(2)}, u32[]{:S(2)}) collective-permute-start(f32[5,80,5,1]{1,2,3,0:T(8,128)} %copy.69), channel_id=1, source_target_pairs={{0,1},{1,2},{2,3},{4,5},{5,6},{6,7},{8,9},{9,10},{10,11},{12,13},{... | collective-permute-start | bytes 24008 | tf_op jit(solution)/shard_map/ppermute | solution.py:26
  78.2 19.6 %copy-start.3 = (f32[5,80,3,384]{3,1,2,0:T(8,128)}, f32[5,80,3,384]{3,1,2,0:T(8,128)S(1)}, u32[]{:S(2)}) copy-start(f32[5,80,3,384]{3,1,2,0:T(8,128)S(1)} %multiply_add_fusion.4) | copy-start | bytes 5529604
  78.3 9.6 %collective-permute-start.4 = (f32[5,80,1,384]{3,1,2,0:T(8,128)S(1)}, f32[5,80,1,384]{3,1,2,0:T(8,128)S(1)}, u32[]{:S(2)}, u32[]{:S(2)}) collective-permute-start(f32[5,80,1,384]{3,1,2,0:T(8,128)S(1)} %get-tuple-element.25), channel_id=1, source_target_pairs={{4,0},{8,4},{12,8},{16,12},{20,16},{24,20},{28,24},{5,1},{9,5},{13... | collective-permute-start | bytes 1843208 | tf_op jit(solution)/shard_map/ppermute | solution.py:27
  80.2 16.3 %collective-permute-start.5 = (f32[5,80,1,384]{3,1,2,0:T(8,128)S(1)}, f32[5,80,1,384]{3,1,2,0:T(8,128)S(1)}, u32[]{:S(2)}, u32[]{:S(2)}) collective-permute-start(f32[5,80,1,384]{3,1,2,0:T(8,128)S(1)} %get-tuple-element.24), channel_id=1, source_target_pairs={{0,4},{4,8},{8,12},{12,16},{16,20},{20,24},{24,28},{1,5},{5,9},{9,... | collective-permute-start | bytes 1843208 | tf_op jit(solution)/shard_map/ppermute | solution.py:26
  96.5 1.3 copy-start.11
  97.8 9.4 %copy-start.17 = (s32[1,1,4]{2,1,0:T(1,128)S(1)}, s32[1,1,4]{2,1,0:T(1,128)}, u32[]{:S(2)}) copy-start(s32[1,1,4]{2,1,0:T(1,128)} %param.19) | copy-start | bytes 52
  97.8 9.4 %copy-start.18 = (s32[1,1,4,4]{3,2,1,0:T(4,128)S(1)}, s32[1,1,4,4]{3,2,1,0:T(4,128)}, u32[]{:S(2)}) copy-start(s32[1,1,4,4]{3,2,1,0:T(4,128)} %param.18) | copy-start | bytes 196
  99.6 12.0 %collective-permute-start.6 = (f32[5,80,5,1]{1,2,3,0:T(8,128)S(1)}, f32[5,80,5,1]{1,2,3,0:T(8,128)S(1)}, u32[]{:S(2)}, u32[]{:S(2)}) collective-permute-start(f32[5,80,5,1]{1,2,3,0:T(8,128)S(1)} %copy.70), channel_id=1, source_target_pairs={{1,0},{2,1},{3,2},{5,4},{6,5},{7,6},{9,8},{10,9},{11,10},{13,12},{... | collective-permute-start | bytes 24008 | tf_op jit(solution)/shard_map/ppermute | solution.py:27
  102.0 10.0 %collective-permute-start.7 = (f32[5,80,5,1]{1,2,3,0:T(8,128)}, f32[5,80,5,1]{1,2,3,0:T(8,128)}, u32[]{:S(2)}, u32[]{:S(2)}) collective-permute-start(f32[5,80,5,1]{1,2,3,0:T(8,128)} %copy.71), channel_id=1, source_target_pairs={{0,1},{1,2},{2,3},{4,5},{5,6},{6,7},{8,9},{9,10},{10,11},{12,13},{... | collective-permute-start | bytes 24008 | tf_op jit(solution)/shard_map/ppermute | solution.py:26
  107.8 22.3 %all-to-all-start = ((s32[4,1,4]{2,1,0:T(1,128)}), s32[4,1,4]{2,1,0:T(1,128)}, u32[]{:S(2)}, u32[]{:S(2)}) async-start(s32[4,1,4]{2,1,0:T(1,128)} %bitcast.4), calls=%async_computation | async-start | bytes 4096 | tf_op jit(solution)/shard_map/all_to_all | solution.py:92
  114.1 7.3 %copy-start.4 = (f32[5,80,3,384]{3,1,2,0:T(8,128)S(1)}, f32[5,80,3,384]{3,1,2,0:T(8,128)}, u32[]{:S(2)}) copy-start(f32[5,80,3,384]{3,1,2,0:T(8,128)} %copy-done.3) | copy-start | bytes 5529604
  114.1 7.4 %copy-start.7 = (f32[5,80,5,1]{3,1,2,0:T(8,128)S(1)}, f32[5,80,5,1]{3,1,2,0:T(8,128)}, u32[]{:S(2)}) copy-start(f32[5,80,5,1]{3,1,2,0:T(8,128)} %copy.59) | copy-start | bytes 24004
  114.1 7.4 %copy-start.12 = (f32[5,80,1,384]{3,1,2,0:T(8,128)S(1)}, f32[5,80,1,384]{3,1,2,0:T(8,128)}, u32[]{:S(2)}) copy-start(f32[5,80,1,384]{3,1,2,0:T(8,128)} %copy-done.11) | copy-start | bytes 1843204
  123.2 1.2 copy-start.1
  124.4 5.5 %copy-start.19 = (s32[1,1,4,4]{3,2,1,0:T(4,128)S(1)}, s32[1,1,4,4]{3,2,1,0:T(4,128)}, u32[]{:S(2)}) copy-start(s32[1,1,4,4]{3,2,1,0:T(4,128)} %param.17) | copy-start | bytes 196
  125.6 9.9 %collective-permute-start.8 = (f32[5,80,1,384]{3,1,2,0:T(8,128)}, f32[5,80,1,384]{3,1,2,0:T(8,128)S(1)}, u32[]{:S(2)}, u32[]{:S(2)}) collective-permute-start(f32[5,80,1,384]{3,1,2,0:T(8,128)} %get-tuple-element.23), channel_id=1, source_target_pairs={{4,0},{8,4},{12,8},{16,12},{20,16},{24,20},{28,24},{5,1},{9,5},{13... | collective-permute-start | bytes 1843208 | tf_op jit(solution)/shard_map/ppermute | solution.py:27
  127.5 16.3 %collective-permute-start.9 = (f32[5,80,1,384]{3,1,2,0:T(8,128)}, f32[5,80,1,384]{3,1,2,0:T(8,128)S(1)}, u32[]{:S(2)}, u32[]{:S(2)}) collective-permute-start(f32[5,80,1,384]{3,1,2,0:T(8,128)} %get-tuple-element.22), channel_id=1, source_target_pairs={{0,4},{4,8},{8,12},{12,16},{16,20},{20,24},{24,28},{1,5},{5,9},{9,... | collective-permute-start | bytes 1843208 | tf_op jit(solution)/shard_map/ppermute | solution.py:26
  132.1 14.9 %copy-start.20 = (s32[16]{0:T(128)}, s32[16]{0:T(128)S(1)}, u32[]{:S(2)}) copy-start(s32[16]{0:T(128)S(1)} %eq.19) | copy-start | bytes 196
  132.2 24.7 %copy-start.24 = (f32[128]{0:T(128)}, f32[128]{0:T(128)S(1)}, u32[]{:S(2)}) copy-start(f32[128]{0:T(128)S(1)} %convert_reduce_fusion) | copy-start | bytes 1540
  143.8 3.2 %copy-start.9 = (f32[5,80,1,384]{3,1,2,0:T(8,128)}, f32[5,80,1,384]{3,1,2,0:T(8,128)S(1)}, u32[]{:S(2)}) copy-start(f32[5,80,1,384]{3,1,2,0:T(8,128)S(1)} %collective-permute-done.9) | copy-start | bytes 1843204
  148.7 8.8 %collective-permute-start.10 = (f32[5,80,5,1]{1,2,3,0:T(8,128)S(1)}, f32[5,80,5,1]{1,2,3,0:T(8,128)S(1)}, u32[]{:S(2)}, u32[]{:S(2)}) collective-permute-start(f32[5,80,5,1]{1,2,3,0:T(8,128)S(1)} %copy.72), channel_id=1, source_target_pairs={{1,0},{2,1},{3,2},{5,4},{6,5},{7,6},{9,8},{10,9},{11,10},{13,12},{... | collective-permute-start | bytes 24008 | tf_op jit(solution)/shard_map/ppermute | solution.py:27
  151.7 6.2 %collective-permute-start.11 = (f32[5,80,5,1]{1,2,3,0:T(8,128)S(1)}, f32[5,80,5,1]{1,2,3,0:T(8,128)}, u32[]{:S(2)}, u32[]{:S(2)}) collective-permute-start(f32[5,80,5,1]{1,2,3,0:T(8,128)S(1)} %copy.73), channel_id=1, source_target_pairs={{0,1},{1,2},{2,3},{4,5},{5,6},{6,7},{8,9},{9,10},{10,11},{12,13},{... | collective-permute-start | bytes 24008 | tf_op jit(solution)/shard_map/ppermute | solution.py:26
  160.0 7.4 %copy-start.2 = (f32[5,80,3,384]{3,1,2,0:T(8,128)S(1)}, f32[5,80,3,384]{3,1,2,0:T(8,128)}, u32[]{:S(2)}) copy-start(f32[5,80,3,384]{3,1,2,0:T(8,128)} %copy-done.1) | copy-start | bytes 5529604
  160.0 7.4 %copy-start.6 = (f32[5,80,5,1]{3,1,2,0:T(8,128)S(1)}, f32[5,80,5,1]{3,1,2,0:T(8,128)}, u32[]{:S(2)}) copy-start(f32[5,80,5,1]{3,1,2,0:T(8,128)} %copy.63) | copy-start | bytes 24004
  160.0 7.4 %copy-start.10 = (f32[5,80,1,384]{3,1,2,0:T(8,128)S(1)}, f32[5,80,1,384]{3,1,2,0:T(8,128)}, u32[]{:S(2)}) copy-start(f32[5,80,1,384]{3,1,2,0:T(8,128)} %copy-done.9) | copy-start | bytes 1843204
  169.1 1.2 copy-start.8
  170.5 8.2 %copy-start.25 = (f32[128]{0:T(128)S(1)}, f32[128]{0:T(128)}, u32[]{:S(2)}) copy-start(f32[128]{0:T(128)} %copy-done.24) | copy-start | bytes 1540
  170.5 13.8 %copy-start.21 = (s32[16]{0:T(128)S(1)}, s32[16]{0:T(128)}, u32[]{:S(2)}) copy-start(s32[16]{0:T(128)} %copy-done.20) | copy-start | bytes 196
  170.6 13.8 %copy-start.22 = (f32[1,128,320]{1,2,0:T(8,128)S(1)}, f32[1,128,320]{1,2,0:T(8,128)}, u32[]{:S(2)}) copy-start(f32[1,128,320]{1,2,0:T(8,128)} %param.16) | copy-start | bytes 491524
  170.6 13.8 %copy-start.26 = (pred[128]{0:T(512)(128)(4,1)S(1)}, pred[128]{0:T(512)(128)(4,1)}, u32[]{:S(2)}) copy-start(pred[128]{0:T(512)(128)(4,1)} %broadcast_compare_fusion) | copy-start | bytes 388
  172.9 11.5 %all-to-all-start.1 = ((f32[4,4,320]{2,1,0:T(4,128)}), f32[4,4,320]{2,1,0:T(4,128)S(1)}, u32[]{:S(2)}, u32[]{:S(2)}) async-start(f32[4,4,320]{2,1,0:T(4,128)} %broadcast_multiply_fusion.3), calls=%async_computation.1 | async-start | bytes 49152 | tf_op jit(solution)/shard_map/all_to_all | solution.py:91
Sparse Core Ops, SparseCore 0:
  17.6 55.9 all-reduce.4
where the time goes:
time: 193 us; the launch traced here: 192 us
  waiting for transfers between devices  72.3 us (37%)
  starting transfers between devices  43.4 us (22%)
  other arithmetic  32 us (17%)
  local copies, waits for them, and re-layouts  28.3 us (15%)
  between operations  15.2 us (8%)
    psum x1, waiting for transfers between devices, broadcast(): return lax.psum(jnp.where(mine, value, jnp.zeros_like(value)), axis)  33.8 us
    ppermute x6, waiting for transfers between devices, padded_2(): before = lax.ppermute(last, axis, up)  24.4 us
    ppermute x6, starting transfers between devices, padded_2(): before = lax.ppermute(last, axis, up)  22.4 us
    add x3, other arithmetic, tendency(): -(wind_east * along_x + wind_north * along_y) + viscosity * spread  18.6 us
    unnamed x62, local copies, waits for them, and re-layouts  13.2 us
    ppermute x6, starting transfers between devices, padded_2(): after = lax.ppermute(leading, axis, down)  11.4 us
    ppermute x6, waiting for transfers between devices, padded_2(): after = lax.ppermute(leading, axis, down)  8.5 us
    ppermute x3, local copies, waits for them, and re-layouts, padded_2(): before = lax.ppermute(last, axis, up)  6.23 us
  transfers between devices with their start and end apart: 15, of which 8 were waited for; matrix products, arithmetic and copies ran while one was open for 15% of the time, Pallas kernels for 0%

commit v1 on v0

--- a/solution.py
+++ b/solution.py
@@ -13,7 +13,7 @@
 
 def broadcast(value, axis, root):
     mine = lax.axis_index(axis) == root
-    return lax.psum(jnp.where(mine, value, jnp.zeros_like(value)), axis)
+    return jnp.sum(lax.all_gather(jnp.where(mine, value, jnp.zeros_like(value)), axis), axis=0)
 
 
 def padded_2(value, sides, width):

time: 193 us -> 179 us (0.927)
  waiting for transfers between devices: 72.3 us -> 57.1 us
  other arithmetic: 32 us -> 35.2 us
  local copies, waits for them, and re-layouts: 28.3 us -> 26.1 us
    psum x1 -> x0, waiting for transfers between devices: 33.8 us -> none  [broadcast(): return lax.psum(jnp.where(mine, value, jnp.zeros_like(value)), axis)]
    all_gather x0 -> x1, waiting for transfers between devices: none -> 12.2 us  [broadcast(): lax.all_gather(jnp.where(mine, value, jnp.zeros_like(value)), axis)]
    ppermute x6, waiting for transfers between devices: 24.4 us -> 29.2 us  [padded_2(): before = lax.ppermute(last, axis, up)]
    reduce_sum x0 -> x1, other arithmetic: none -> 2.72 us  [broadcast(): jnp.sum(lax.all_gather(jnp.where(mine, value, jnp.zeros_like(value)), axi...]
    slice x4, local copies, waits for them, and re-layouts: 5.19 us -> 2.8 us  [padded_2(): last = lax.slice_in_dim(value, length - width, length, axis=dim)]
    unnamed x62 -> x66, local copies, waits for them, and re-layouts: 13.2 us -> 13.3 us
  transfers between devices with their start and end apart: 15 -> 15, of which waited for: 8 -> 9; matrix products, arithmetic and copies ran while one was open for 15% -> 14% of each run, Pallas kernels for 0% -> 0%
where the time goes in v1:
time: 179 us; the launch traced here: 178 us
  waiting for transfers between devices  57.1 us (32%)
  starting transfers between devices  43.4 us (24%)
  other arithmetic  35.2 us (20%)
  local copies, waits for them, and re-layouts  26.1 us (15%)
  between operations  15.3 us (9%)
    ppermute x6, waiting for transfers between devices, padded_2(): before = lax.ppermute(last, axis, up)  29.2 us
    ppermute x6, starting transfers between devices, padded_2(): before = lax.ppermute(last, axis, up)  21.2 us
    add x3, other arithmetic, tendency(): -(wind_east * along_x + wind_north * along_y) + viscosity * spread  19.3 us
    unnamed x66, local copies, waits for them, and re-layouts  13.3 us
    ppermute x6, starting transfers between devices, padded_2(): after = lax.ppermute(leading, axis, down)  12.5 us
    all_gather x1, waiting for transfers between devices, broadcast(): lax.all_gather(jnp.where(mine, value, jnp.zeros_like(value)), axis)  12.2 us
    ppermute x6, waiting for transfers between devices, padded_2(): after = lax.ppermute(leading, axis, down)  10.1 us
    all_to_all x1, starting transfers between devices, on_device(): lax.all_to_all(records, 'gy', split_axis=0, concat_axis=0, tiled=True)  5.88 us
  transfers between devices with their start and end apart: 15, of which 9 were waited for; matrix products, arithmetic and copies ran while one was open for 14% of the time, Pallas kernels for 0%

profile of v1, /device:TPU:6, one launch (start us, length us, event | category | flops | bytes accessed | tf_op | source)
XLA Modules:
  0.0 178.0 jit_solution(4432876079178400170)
XLA Ops:
  7.2 1.4 dynamic_slice.3
  9.2 0.9 broadcast_select_fusion
  10.2 1.9 %collective-permute-start.1 = (f32[5,80,1,384]{3,1,2,0:T(8,128)S(1)}, f32[5,80,1,384]{3,1,2,0:T(8,128)S(1)}, u32[]{:S(2)}, u32[]{:S(2)}) collective-permute-start(f32[5,80,1,384]{3,1,2,0:T(8,128)S(1)} %get-tuple-element.26), channel_id=1, source_target_pairs={{0,4},{4,8},{8,12},{12,16},{16,20},{20,24},{24,28},{1,5},{5,9},{9,... | collective-permute-start | bytes 1843208 | tf_op jit(solution)/shard_map/ppermute | solution.py:26
  12.2 3.6 %collective-permute-start = (f32[5,80,1,384]{3,1,2,0:T(8,128)S(1)}, f32[5,80,1,384]{3,1,2,0:T(8,128)S(1)}, u32[]{:S(2)}, u32[]{:S(2)}) collective-permute-start(f32[5,80,1,384]{3,1,2,0:T(8,128)S(1)} %get-tuple-element.27), channel_id=1, source_target_pairs={{4,0},{8,4},{12,8},{16,12},{20,16},{24,20},{28,24},{5,1},{9,5},{13... | collective-permute-start | bytes 1843208 | tf_op jit(solution)/shard_map/ppermute | solution.py:27
  15.8 11.8 %collective-permute-done.1 = f32[5,80,1,384]{3,1,2,0:T(8,128)S(1)} collective-permute-done((f32[5,80,1,384]{3,1,2,0:T(8,128)S(1)}, f32[5,80,1,384]{3,1,2,0:T(8,128)S(1)}, u32[]{:S(2)}, u32[]{:S(2)}) %collective-permute-start.1) | collective-permute-done | bytes 614432 | tf_op jit(solution)/shard_map/ppermute | solution.py:26
  28.5 1.1 collective-permute-done
  29.6 0.9 copy-done.16
  30.5 1.5 fusion.36
  32.5 1.7 copy.67
  34.2 1.3 collective-permute-start.2
  36.0 4.6 %collective-permute-start.3 = (f32[5,80,5,1]{1,2,3,0:T(8,128)S(1)}, f32[5,80,5,1]{1,2,3,0:T(8,128)S(1)}, u32[]{:S(2)}, u32[]{:S(2)}) collective-permute-start(f32[5,80,5,1]{1,2,3,0:T(8,128)S(1)} %copy.68), channel_id=1, source_target_pairs={{0,1},{1,2},{2,3},{4,5},{5,6},{6,7},{8,9},{9,10},{10,11},{12,13},{... | collective-permute-start | bytes 24008 | tf_op jit(solution)/shard_map/ppermute | solution.py:26
  41.0 1.0 collective-permute-done.3
  42.1 1.3 copy.54
  43.4 12.2 %all-gather.3.cloned.1.call-done = f32[8,5,80,384]{3,2,1,0:T(8,128)} async-done(((f32[1,5,80,384]{3,2,1,0:T(8,128)}), f32[8,5,80,384]{3,2,1,0:T(8,128)}) %all-gather.3.cloned.1.call-update) | async-done | bytes 4915216 | tf_op jit(solution)/shard_map/all_gather | solution.py:16
  55.6 2.7 %reduce.4 = f32[5,80,384]{2,1,0:T(8,128)S(1)} reduce(f32[8,5,80,384]{3,2,1,0:T(8,128)} %all-gather.3.cloned.1.call-done, f32[]{:T(128)} %constant.18.clone.1), dimensions={0}, to_apply=%region_0.1 | reduce | flops 1075200 | bytes 5529604 | tf_op jit(solution)/shard_map/reduce_sum | solution.py:16
  58.4 4.1 %multiply_add_fusion.5 = (f32[5,80,3,384]{3,1,2,0:T(8,128)S(1)}, f32[5,80,3,384]{3,1,2,0:T(8,128)S(1)}, f32[5,80,3,384]{3,1,2,0:T(8,128)S(1)}, f32[5,80,3,384]{3,1,2,0:T(8,128)S(1)}) fusion(f32[5,80,3,384]{3,1,2,0:T(8,128)S(1)} %copy-done, f32[5,80,1,384]{3,1,2,0:T(8,128)} %copy-done.16, f32[5,80,1,384]{3,1,2,0:T(8,128)} %copy-done.15, ...), kind=kLoop, calls=%fused_computation.40 | loop fusion | flops 11980800 | bytes 14161024 | tf_op jit(solution)/shard_map/add | solution.py:44
  63.1 3.0 %collective-permute-start.4 = (f32[5,80,1,384]{3,1,2,0:T(8,128)S(1)}, f32[5,80,1,384]{3,1,2,0:T(8,128)S(1)}, u32[]{:S(2)}, u32[]{:S(2)}) collective-permute-start(f32[5,80,1,384]{3,1,2,0:T(8,128)S(1)} %get-tuple-element.25), channel_id=1, source_target_pairs={{4,0},{8,4},{12,8},{16,12},{20,16},{24,20},{28,24},{5,1},{9,5},{13... | collective-permute-start | bytes 1843208 | tf_op jit(solution)/shard_map/ppermute | solution.py:27
  66.2 1.9 %collective-permute-start.5 = (f32[5,80,1,384]{3,1,2,0:T(8,128)S(1)}, f32[5,80,1,384]{3,1,2,0:T(8,128)S(1)}, u32[]{:S(2)}, u32[]{:S(2)}) collective-permute-start(f32[5,80,1,384]{3,1,2,0:T(8,128)S(1)} %get-tuple-element.24), channel_id=1, source_target_pairs={{0,4},{4,8},{8,12},{12,16},{16,20},{20,24},{24,28},{1,5},{5,9},{9,... | collective-permute-start | bytes 1843208 | tf_op jit(solution)/shard_map/ppermute | solution.py:26
  68.1 5.7 %collective-permute-done.4 = f32[5,80,1,384]{3,1,2,0:T(8,128)S(1)} collective-permute-done((f32[5,80,1,384]{3,1,2,0:T(8,128)S(1)}, f32[5,80,1,384]{3,1,2,0:T(8,128)S(1)}, u32[]{:S(2)}, u32[]{:S(2)}) %collective-permute-start.4) | collective-permute-done | bytes 614432 | tf_op jit(solution)/shard_map/ppermute | solution.py:27
  73.8 8.7 %collective-permute-done.5 = f32[5,80,1,384]{3,1,2,0:T(8,128)S(1)} collective-permute-done((f32[5,80,1,384]{3,1,2,0:T(8,128)S(1)}, f32[5,80,1,384]{3,1,2,0:T(8,128)S(1)}, u32[]{:S(2)}, u32[]{:S(2)}) %collective-permute-start.5) | collective-permute-done | bytes 614432 | tf_op jit(solution)/shard_map/ppermute | solution.py:26
  82.5 1.3 pad_maximum_fusion.23
  83.9 1.7 copy.69
  85.6 1.3 collective-permute-start.6
  86.9 1.1 copy.70
  88.1 5.1 %collective-permute-start.7 = (f32[5,80,5,1]{1,2,3,0:T(8,128)}, f32[5,80,5,1]{1,2,3,0:T(8,128)}, u32[]{:S(2)}, u32[]{:S(2)}) collective-permute-start(f32[5,80,5,1]{1,2,3,0:T(8,128)} %copy.70), channel_id=1, source_target_pairs={{0,1},{1,2},{2,3},{4,5},{5,6},{6,7},{8,9},{9,10},{10,11},{12,13},{... | collective-permute-start | bytes 24008 | tf_op jit(solution)/shard_map/ppermute | solution.py:26
  93.9 3.8 %all-to-all-start = ((s32[4,1,4]{2,1,0:T(1,128)}), s32[4,1,4]{2,1,0:T(1,128)}, u32[]{:S(2)}, u32[]{:S(2)}) async-start(s32[4,1,4]{2,1,0:T(1,128)} %bitcast.3), calls=%async_computation | async-start | bytes 4096 | tf_op jit(solution)/shard_map/all_to_all | solution.py:92
  98.1 2.1 %copy.58 = f32[5,80,5,1]{3,1,2,0:T(8,128)} copy(f32[5,80,5,1]{1,2,3,0:T(8,128)} %collective-permute-done.7) | data formatting | bytes 16000 | tf_op jit(solution)/shard_map/ppermute | solution.py:26
  100.2 7.6 %multiply_add_fusion.3 = (f32[5,80,3,384]{3,1,2,0:T(8,128)S(1)}, f32[5,80,3,384]{3,1,2,0:T(8,128)S(1)}, f32[5,80,3,384]{3,1,2,0:T(8,128)S(1)}) fusion(f32[5,80,3,384]{3,1,2,0:T(8,128)} %copy-done.3, f32[5,80,1,384]{3,1,2,0:T(8,128)} %copy-done.11, f32[5,80,1,384]{3,1,2,0:T(8,128)} %copy-done.13, f32[5,80,384]{2,1,0:T(8,128)S(1)} %reduce.4, ...), kind=kLoop, calls=%fused_computation.37 | loop fusion | flops 13363200 | bytes 9245824 | tf_op jit(solution)/shard_map/add | solution.py:44
  107.9 1.2 broadcast_multiply_fusion.1
  109.6 1.2 copy-done.1
  110.8 1.1 fusion.38
  111.9 1.9 %collective-permute-start.8 = (f32[5,80,1,384]{3,1,2,0:T(8,128)}, f32[5,80,1,384]{3,1,2,0:T(8,128)S(1)}, u32[]{:S(2)}, u32[]{:S(2)}) collective-permute-start(f32[5,80,1,384]{3,1,2,0:T(8,128)} %get-tuple-element.23), channel_id=1, source_target_pairs={{4,0},{8,4},{12,8},{16,12},{20,16},{24,20},{28,24},{5,1},{9,5},{13... | collective-permute-start | bytes 1843208 | tf_op jit(solution)/shard_map/ppermute | solution.py:27
  113.9 2.4 %collective-permute-start.9 = (f32[5,80,1,384]{3,1,2,0:T(8,128)}, f32[5,80,1,384]{3,1,2,0:T(8,128)}, u32[]{:S(2)}, u32[]{:S(2)}) collective-permute-start(f32[5,80,1,384]{3,1,2,0:T(8,128)} %get-tuple-element.22), channel_id=1, source_target_pairs={{0,4},{4,8},{8,12},{12,16},{16,20},{20,24},{24,28},{1,5},{5,9},{9,... | collective-permute-start | bytes 1843208 | tf_op jit(solution)/shard_map/ppermute | solution.py:26
  117.0 1.3 reduce.9
  118.5 3.3 %collective-permute-done.8 = f32[5,80,1,384]{3,1,2,0:T(8,128)S(1)} collective-permute-done((f32[5,80,1,384]{3,1,2,0:T(8,128)}, f32[5,80,1,384]{3,1,2,0:T(8,128)S(1)}, u32[]{:S(2)}, u32[]{:S(2)}) %collective-permute-start.8) | collective-permute-done | bytes 614432 | tf_op jit(solution)/shard_map/ppermute | solution.py:27
  121.8 7.6 %collective-permute-done.9 = f32[5,80,1,384]{3,1,2,0:T(8,128)} collective-permute-done((f32[5,80,1,384]{3,1,2,0:T(8,128)}, f32[5,80,1,384]{3,1,2,0:T(8,128)}, u32[]{:S(2)}, u32[]{:S(2)}) %collective-permute-start.9) | collective-permute-done | bytes 614432 | tf_op jit(solution)/shard_map/ppermute | solution.py:26
  129.4 3.0 %pad_maximum_fusion.20 = (f32[5,80,5,1]{3,1,2,0:T(8,128)}, f32[5,80,5,1]{3,1,2,0:T(8,128)}) fusion(f32[5,80,1,384]{3,1,2,0:T(8,128)S(1)} %collective-permute-done.8, f32[5,80,3,384]{3,1,2,0:T(8,128)} %copy-done.1, f32[5,80,1,384]{3,1,2,0:T(8,128)} %collective-permute-done.9), kind=kLoop, calls=%fused_computation.46 | loop fusion | flops 8000 | bytes 3088000 | tf_op jit(solution)/shard_map/concatenate | solution.py:28
  132.5 1.7 copy.71
  134.2 1.3 collective-permute-start.10
  135.5 1.7 copy.72
  137.2 5.2 %collective-permute-start.11 = (f32[5,80,5,1]{1,2,3,0:T(8,128)S(1)}, f32[5,80,5,1]{1,2,3,0:T(8,128)}, u32[]{:S(2)}, u32[]{:S(2)}) collective-permute-start(f32[5,80,5,1]{1,2,3,0:T(8,128)S(1)} %copy.72), channel_id=1, source_target_pairs={{0,1},{1,2},{2,3},{4,5},{5,6},{6,7},{8,9},{9,10},{10,11},{12,13},{... | collective-permute-start | bytes 24008 | tf_op jit(solution)/shard_map/ppermute | solution.py:26
  143.4 2.1 %copy.62 = f32[5,80,5,1]{3,1,2,0:T(8,128)} copy(f32[5,80,5,1]{1,2,3,0:T(8,128)} %collective-permute-done.11) | data formatting | bytes 16000 | tf_op jit(solution)/shard_map/ppermute | solution.py:26
  145.5 7.6 %multiply_add_fusion.1 = (f32[5,80,3,384]{3,1,2,0:T(8,128)S(1)}, f32[5,80,3,384]{3,1,2,0:T(8,128)S(1)}, f32[5,80,3,384]{3,1,2,0:T(8,128)S(1)}) fusion(f32[5,80,3,384]{3,1,2,0:T(8,128)} %copy-done.1, f32[5,80,1,384]{3,1,2,0:T(8,128)} %copy-done.9, f32[5,80,1,384]{3,1,2,0:T(8,128)} %collective-permute-done.9, f32[5,80,384]{2,1,0:T(8,128)S(1)} %reduce.4, ...), kind=kLoop, calls=%fused_computation.34 | loop fusion | flops 13363200 | bytes 9245824 | tf_op jit(solution)/shard_map/add | solution.py:44
  153.1 1.2 broadcast_multiply_fusion
  154.9 1.2 copy-done.8
  158.6 5.9 %all-to-all-start.1 = ((f32[4,4,320]{2,1,0:T(4,128)}), f32[4,4,320]{2,1,0:T(4,128)S(1)}, u32[]{:S(2)}, u32[]{:S(2)}) async-start(f32[4,4,320]{2,1,0:T(4,128)} %broadcast_multiply_fusion.3), calls=%async_computation.1 | async-start | bytes 49152 | tf_op jit(solution)/shard_map/all_to_all | solution.py:91
  164.5 5.6 %all-to-all-done.1 = f32[4,4,320]{2,1,0:T(4,128)S(1)} async-done(((f32[4,4,320]{2,1,0:T(4,128)}), f32[4,4,320]{2,1,0:T(4,128)S(1)}, u32[]{:S(2)}, u32[]{:S(2)}) %all-to-all-start.1) | async-done | bytes 20512 | tf_op jit(solution)/shard_map/all_to_all | solution.py:91
  170.2 1.0 fusion.7
  (112 shorter events, 9.4 us)
Async XLA Ops:
  7.2 3.0 %copy-start = (f32[5,80,3,384]{3,1,2,0:T(8,128)S(1)}, f32[5,80,3,384]{3,1,2,0:T(8,128)}, u32[]{:S(2)}) copy-start(f32[5,80,3,384]{3,1,2,0:T(8,128)} %param.10) | copy-start | bytes 5529604
  7.2 48.5 %all-gather.3.cloned.1.call-start = ((), (), s32[]{:S(2)}) async-start(), calls=%async_computation.2 | async-start | bytes 5529600 | tf_op jit(solution)/shard_map/all_gather | solution.py:16
  10.2 17.4 %collective-permute-start.1 = (f32[5,80,1,384]{3,1,2,0:T(8,128)S(1)}, f32[5,80,1,384]{3,1,2,0:T(8,128)S(1)}, u32[]{:S(2)}, u32[]{:S(2)}) collective-permute-start(f32[5,80,1,384]{3,1,2,0:T(8,128)S(1)} %get-tuple-element.26), channel_id=1, source_target_pairs={{0,4},{4,8},{8,12},{12,16},{16,20},{20,24},{24,28},{1,5},{5,9},{9,... | collective-permute-start | bytes 1843208 | tf_op jit(solution)/shard_map/ppermute | solution.py:26
  12.2 17.4 %collective-permute-start = (f32[5,80,1,384]{3,1,2,0:T(8,128)S(1)}, f32[5,80,1,384]{3,1,2,0:T(8,128)S(1)}, u32[]{:S(2)}, u32[]{:S(2)}) collective-permute-start(f32[5,80,1,384]{3,1,2,0:T(8,128)S(1)} %get-tuple-element.27), channel_id=1, source_target_pairs={{4,0},{8,4},{12,8},{16,12},{20,16},{24,20},{28,24},{5,1},{9,5},{13... | collective-permute-start | bytes 1843208 | tf_op jit(solution)/shard_map/ppermute | solution.py:27
  27.6 0.8 copy-start.15
  29.5 0.9 copy-start.16
  30.5 2.0 %copy-start.5 = (f32[5,80,5,384]{3,1,2,0:T(8,128)}, f32[5,80,5,384]{3,1,2,0:T(8,128)S(1)}, u32[]{:S(2)}) copy-start(f32[5,80,5,384]{3,1,2,0:T(8,128)S(1)} %constant_dynamic-update-slice_fusion) | copy-start | bytes 9216004
  32.5 8.1 %copy-start.19 = (f32[3,384]{1,0:T(4,128)S(1)}, f32[3,384]{1,0:T(4,128)}, u32[]{:S(2)}) copy-start(f32[3,384]{1,0:T(4,128)} %param.14) | copy-start | bytes 13828
  34.2 6.4 %collective-permute-start.2 = (f32[5,80,5,1]{1,2,3,0:T(8,128)S(1)}, f32[5,80,5,1]{1,2,3,0:T(8,128)S(1)}, u32[]{:S(2)}, u32[]{:S(2)}) collective-permute-start(f32[5,80,5,1]{1,2,3,0:T(8,128)S(1)} %copy.67), channel_id=1, source_target_pairs={{1,0},{2,1},{3,2},{5,4},{6,5},{7,6},{9,8},{10,9},{11,10},{13,12},{... | collective-permute-start | bytes 24008 | tf_op jit(solution)/shard_map/ppermute | solution.py:27
  36.0 6.0 %collective-permute-start.3 = (f32[5,80,5,1]{1,2,3,0:T(8,128)S(1)}, f32[5,80,5,1]{1,2,3,0:T(8,128)S(1)}, u32[]{:S(2)}, u32[]{:S(2)}) collective-permute-start(f32[5,80,5,1]{1,2,3,0:T(8,128)S(1)} %copy.68), channel_id=1, source_target_pairs={{0,1},{1,2},{2,3},{4,5},{5,6},{6,7},{8,9},{9,10},{10,11},{12,13},{... | collective-permute-start | bytes 24008 | tf_op jit(solution)/shard_map/ppermute | solution.py:26
  43.4 14.9 %copy-start.17 = (f32[3,384]{1,0:T(4,128)S(1)}, f32[3,384]{1,0:T(4,128)}, u32[]{:S(2)}) copy-start(f32[3,384]{1,0:T(4,128)} %param.15) | copy-start | bytes 13828
  43.4 14.9 %copy-start.18 = (f32[3,384]{1,0:T(4,128)S(1)}, f32[3,384]{1,0:T(4,128)}, u32[]{:S(2)}) copy-start(f32[3,384]{1,0:T(4,128)} %param.13) | copy-start | bytes 13828
  63.0 20.8 %copy-start.3 = (f32[5,80,3,384]{3,1,2,0:T(8,128)}, f32[5,80,3,384]{3,1,2,0:T(8,128)S(1)}, u32[]{:S(2)}) copy-start(f32[5,80,3,384]{3,1,2,0:T(8,128)S(1)} %multiply_add_fusion.4) | copy-start | bytes 5529604
  63.1 10.7 %collective-permute-start.4 = (f32[5,80,1,384]{3,1,2,0:T(8,128)S(1)}, f32[5,80,1,384]{3,1,2,0:T(8,128)S(1)}, u32[]{:S(2)}, u32[]{:S(2)}) collective-permute-start(f32[5,80,1,384]{3,1,2,0:T(8,128)S(1)} %get-tuple-element.25), channel_id=1, source_target_pairs={{4,0},{8,4},{12,8},{16,12},{20,16},{24,20},{28,24},{5,1},{9,5},{13... | collective-permute-start | bytes 1843208 | tf_op jit(solution)/shard_map/ppermute | solution.py:27
  66.2 16.3 %collective-permute-start.5 = (f32[5,80,1,384]{3,1,2,0:T(8,128)S(1)}, f32[5,80,1,384]{3,1,2,0:T(8,128)S(1)}, u32[]{:S(2)}, u32[]{:S(2)}) collective-permute-start(f32[5,80,1,384]{3,1,2,0:T(8,128)S(1)} %get-tuple-element.24), channel_id=1, source_target_pairs={{0,4},{4,8},{8,12},{12,16},{16,20},{20,24},{24,28},{1,5},{5,9},{9,... | collective-permute-start | bytes 1843208 | tf_op jit(solution)/shard_map/ppermute | solution.py:26
  73.8 10.0 %copy-start.11 = (f32[5,80,1,384]{3,1,2,0:T(8,128)}, f32[5,80,1,384]{3,1,2,0:T(8,128)S(1)}, u32[]{:S(2)}) copy-start(f32[5,80,1,384]{3,1,2,0:T(8,128)S(1)} %collective-permute-done.4) | copy-start | bytes 1843204
  82.5 1.3 copy-start.13
  83.9 9.3 %copy-start.20 = (s32[1,1,4]{2,1,0:T(1,128)S(1)}, s32[1,1,4]{2,1,0:T(1,128)}, u32[]{:S(2)}) copy-start(s32[1,1,4]{2,1,0:T(1,128)} %param.19) | copy-start | bytes 52
  83.9 9.3 %copy-start.21 = (s32[1,1,4,4]{3,2,1,0:T(4,128)S(1)}, s32[1,1,4,4]{3,2,1,0:T(4,128)}, u32[]{:S(2)}) copy-start(s32[1,1,4,4]{3,2,1,0:T(4,128)} %param.18) | copy-start | bytes 196
  85.6 12.0 %collective-permute-start.6 = (f32[5,80,5,1]{1,2,3,0:T(8,128)S(1)}, f32[5,80,5,1]{1,2,3,0:T(8,128)S(1)}, u32[]{:S(2)}, u32[]{:S(2)}) collective-permute-start(f32[5,80,5,1]{1,2,3,0:T(8,128)S(1)} %copy.69), channel_id=1, source_target_pairs={{1,0},{2,1},{3,2},{5,4},{6,5},{7,6},{9,8},{10,9},{11,10},{13,12},{... | collective-permute-start | bytes 24008 | tf_op jit(solution)/shard_map/ppermute | solution.py:27
  88.1 10.0 %collective-permute-start.7 = (f32[5,80,5,1]{1,2,3,0:T(8,128)}, f32[5,80,5,1]{1,2,3,0:T(8,128)}, u32[]{:S(2)}, u32[]{:S(2)}) collective-permute-start(f32[5,80,5,1]{1,2,3,0:T(8,128)} %copy.70), channel_id=1, source_target_pairs={{0,1},{1,2},{2,3},{4,5},{5,6},{6,7},{8,9},{9,10},{10,11},{12,13},{... | collective-permute-start | bytes 24008 | tf_op jit(solution)/shard_map/ppermute | solution.py:26
  93.9 22.6 %all-to-all-start = ((s32[4,1,4]{2,1,0:T(1,128)}), s32[4,1,4]{2,1,0:T(1,128)}, u32[]{:S(2)}, u32[]{:S(2)}) async-start(s32[4,1,4]{2,1,0:T(1,128)} %bitcast.3), calls=%async_computation | async-start | bytes 4096 | tf_op jit(solution)/shard_map/all_to_all | solution.py:92
  100.1 7.7 %copy-start.4 = (f32[5,80,3,384]{3,1,2,0:T(8,128)S(1)}, f32[5,80,3,384]{3,1,2,0:T(8,128)}, u32[]{:S(2)}) copy-start(f32[5,80,3,384]{3,1,2,0:T(8,128)} %copy-done.3) | copy-start | bytes 5529604
  100.1 7.7 %copy-start.7 = (f32[5,80,5,1]{3,1,2,0:T(8,128)S(1)}, f32[5,80,5,1]{3,1,2,0:T(8,128)}, u32[]{:S(2)}) copy-start(f32[5,80,5,1]{3,1,2,0:T(8,128)} %copy.58) | copy-start | bytes 24004
  100.1 7.7 %copy-start.12 = (f32[5,80,1,384]{3,1,2,0:T(8,128)S(1)}, f32[5,80,1,384]{3,1,2,0:T(8,128)}, u32[]{:S(2)}) copy-start(f32[5,80,1,384]{3,1,2,0:T(8,128)} %copy-done.11) | copy-start | bytes 1843204
  100.2 7.7 %copy-start.14 = (f32[5,80,1,384]{3,1,2,0:T(8,128)S(1)}, f32[5,80,1,384]{3,1,2,0:T(8,128)}, u32[]{:S(2)}) copy-start(f32[5,80,1,384]{3,1,2,0:T(8,128)} %copy-done.13) | copy-start | bytes 1843204
  109.6 1.2 copy-start.1
  110.8 5.5 %copy-start.22 = (s32[1,1,4,4]{3,2,1,0:T(4,128)S(1)}, s32[1,1,4,4]{3,2,1,0:T(4,128)}, u32[]{:S(2)}) copy-start(s32[1,1,4,4]{3,2,1,0:T(4,128)} %param.17) | copy-start | bytes 196
  111.9 9.9 %collective-permute-start.8 = (f32[5,80,1,384]{3,1,2,0:T(8,128)}, f32[5,80,1,384]{3,1,2,0:T(8,128)S(1)}, u32[]{:S(2)}, u32[]{:S(2)}) collective-permute-start(f32[5,80,1,384]{3,1,2,0:T(8,128)} %get-tuple-element.23), channel_id=1, source_target_pairs={{4,0},{8,4},{12,8},{16,12},{20,16},{24,20},{28,24},{5,1},{9,5},{13... | collective-permute-start | bytes 1843208 | tf_op jit(solution)/shard_map/ppermute | solution.py:27
  113.9 15.6 %collective-permute-start.9 = (f32[5,80,1,384]{3,1,2,0:T(8,128)}, f32[5,80,1,384]{3,1,2,0:T(8,128)}, u32[]{:S(2)}, u32[]{:S(2)}) collective-permute-start(f32[5,80,1,384]{3,1,2,0:T(8,128)} %get-tuple-element.22), channel_id=1, source_target_pairs={{0,4},{4,8},{8,12},{12,16},{16,20},{20,24},{24,28},{1,5},{5,9},{9,... | collective-permute-start | bytes 1843208 | tf_op jit(solution)/shard_map/ppermute | solution.py:26
  118.4 14.0 %copy-start.23 = (s32[16]{0:T(128)}, s32[16]{0:T(128)S(1)}, u32[]{:S(2)}) copy-start(s32[16]{0:T(128)S(1)} %eq.19) | copy-start | bytes 196
  118.5 23.9 %copy-start.26 = (f32[128]{0:T(128)}, f32[128]{0:T(128)S(1)}, u32[]{:S(2)}) copy-start(f32[128]{0:T(128)S(1)} %convert_reduce_fusion) | copy-start | bytes 1540
  121.8 10.6 %copy-start.9 = (f32[5,80,1,384]{3,1,2,0:T(8,128)}, f32[5,80,1,384]{3,1,2,0:T(8,128)S(1)}, u32[]{:S(2)}) copy-start(f32[5,80,1,384]{3,1,2,0:T(8,128)S(1)} %collective-permute-done.8) | copy-start | bytes 1843204
  134.2 8.8 %collective-permute-start.10 = (f32[5,80,5,1]{1,2,3,0:T(8,128)S(1)}, f32[5,80,5,1]{1,2,3,0:T(8,128)S(1)}, u32[]{:S(2)}, u32[]{:S(2)}) collective-permute-start(f32[5,80,5,1]{1,2,3,0:T(8,128)S(1)} %copy.71), channel_id=1, source_target_pairs={{1,0},{2,1},{3,2},{5,4},{6,5},{7,6},{9,8},{10,9},{11,10},{13,12},{... | collective-permute-start | bytes 24008 | tf_op jit(solution)/shard_map/ppermute | solution.py:27
  137.2 6.1 %collective-permute-start.11 = (f32[5,80,5,1]{1,2,3,0:T(8,128)S(1)}, f32[5,80,5,1]{1,2,3,0:T(8,128)}, u32[]{:S(2)}, u32[]{:S(2)}) collective-permute-start(f32[5,80,5,1]{1,2,3,0:T(8,128)S(1)} %copy.72), channel_id=1, source_target_pairs={{0,1},{1,2},{2,3},{4,5},{5,6},{6,7},{8,9},{9,10},{10,11},{12,13},{... | collective-permute-start | bytes 24008 | tf_op jit(solution)/shard_map/ppermute | solution.py:26
  145.5 7.7 %copy-start.2 = (f32[5,80,3,384]{3,1,2,0:T(8,128)S(1)}, f32[5,80,3,384]{3,1,2,0:T(8,128)}, u32[]{:S(2)}) copy-start(f32[5,80,3,384]{3,1,2,0:T(8,128)} %copy-done.1) | copy-start | bytes 5529604
  145.5 7.7 %copy-start.6 = (f32[5,80,5,1]{3,1,2,0:T(8,128)S(1)}, f32[5,80,5,1]{3,1,2,0:T(8,128)}, u32[]{:S(2)}) copy-start(f32[5,80,5,1]{3,1,2,0:T(8,128)} %copy.62) | copy-start | bytes 24004
  145.5 7.7 %copy-start.10 = (f32[5,80,1,384]{3,1,2,0:T(8,128)S(1)}, f32[5,80,1,384]{3,1,2,0:T(8,128)}, u32[]{:S(2)}) copy-start(f32[5,80,1,384]{3,1,2,0:T(8,128)} %copy-done.9) | copy-start | bytes 1843204
  154.9 1.2 copy-start.8
  156.3 8.2 %copy-start.27 = (f32[128]{0:T(128)S(1)}, f32[128]{0:T(128)}, u32[]{:S(2)}) copy-start(f32[128]{0:T(128)} %copy-done.26) | copy-start | bytes 1540
  156.3 13.9 %copy-start.24 = (s32[16]{0:T(128)S(1)}, s32[16]{0:T(128)}, u32[]{:S(2)}) copy-start(s32[16]{0:T(128)} %copy-done.23) | copy-start | bytes 196
  156.3 13.9 %copy-start.25 = (f32[1,128,320]{1,2,0:T(8,128)S(1)}, f32[1,128,320]{1,2,0:T(8,128)}, u32[]{:S(2)}) copy-start(f32[1,128,320]{1,2,0:T(8,128)} %param.16) | copy-start | bytes 491524
  156.3 13.9 %copy-start.28 = (pred[128]{0:T(512)(128)(4,1)S(1)}, pred[128]{0:T(512)(128)(4,1)}, u32[]{:S(2)}) copy-start(pred[128]{0:T(512)(128)(4,1)} %broadcast_compare_fusion) | copy-start | bytes 388
  158.6 11.5 %all-to-all-start.1 = ((f32[4,4,320]{2,1,0:T(4,128)}), f32[4,4,320]{2,1,0:T(4,128)S(1)}, u32[]{:S(2)}, u32[]{:S(2)}) async-start(f32[4,4,320]{2,1,0:T(4,128)} %broadcast_multiply_fusion.3), calls=%async_computation.1 | async-start | bytes 49152 | tf_op jit(solution)/shard_map/all_to_all | solution.py:91
Sparse Core Ops, SparseCore 0:
  10.2 45.3 all-gather.2
